TPU v7x, 32 devices: a whole 2x2x4 slice. The times are simulated.
32 devices in a mesh: dp: 2 (over core), pipe: 2 (over x), ctx: 8 (over z, y).
Axes of the slice: x: 2, y: 2, z: 4, core: 2. Of those that a mesh axis runs over, the one named last changes fastest.
Arguments:
- queries: bfloat16 [4, 1024, 2048], P(('dp', 'pipe'), 'ctx'), parts along dimension 0, may hold values from -6 to 6
- section_key_state: bfloat16 [4, 1024, 256], P(('dp', 'pipe'), 'ctx'), parts along dimension 0, may hold values from -6 to 6
- section_value_state: bfloat16 [4, 1024, 256], P(('dp', 'pipe'), 'ctx'), parts along dimension 0, may hold values from -6 to 6
- out_grad: bfloat16 [4, 1024, 2048], P(('dp', 'pipe'), 'ctx'), parts along dimension 0, may hold values from -6 to 6
- doc_blocks: int32 [4, 4], P(('dp', 'pipe')), parts along dimension 0, may hold values from 1 to 4, 8 in all within a row
Outputs:
- attention: bfloat16 [4, 1024, 2048], P(('dp', 'pipe'), 'ctx'), parts along dimension 0
- query_grads: bfloat16 [4, 1024, 2048], P(('dp', 'pipe'), 'ctx'), parts along dimension 0
- key_grads: bfloat16 [4, 1024, 256], P(('dp', 'pipe'), 'ctx'), parts along dimension 0
- value_grads: bfloat16 [4, 1024, 256], P(('dp', 'pipe'), 'ctx'), parts along dimension 0
There are 2 independent parts, one for each index of `dp`. A program takes and returns all parts, laid end to end along the dimension named above; each array names one. Nothing has to cross between parts.
Inputs may be any that keep to these rules, and one draw needn't show every extreme that they name: `doc_blocks`: each row sums to 8, and one document of each row has exactly 4 blocks.
All inputs are finite; a program needn't handle non-finite values.
Results may differ from a plain program's by a relative error of at most 0.012.
The roundings to bfloat16 on the way count: a program that leaves them out, or rounds other values in their place, can miss the bound.
Values may be sent and summed in bfloat16 or wider, within the bound.
A program may use at most 64 MiB of HBM per device.

v0:
```python
import math
import jax
import jax.numpy as jnp
from jax import lax
from jax.sharding import PartitionSpec as P

QUERY_HEAD_COUNT = 16
KEY_VALUE_HEADS = 2
HEAD_SIZE = 128
BLK = 128


def from_behind(x, axis, by):
    length = lax.axis_size(axis)
    pairs = [(i, i + by) for i in range(length) if 0 <= i + by < length]
    return lax.ppermute(x, axis, pairs)


def layout_positions(device_at, shard_rows, shard_count):
    half_rows = shard_rows // 2
    offsets = jnp.arange(half_rows, dtype=jnp.int32)
    lower_half = device_at * half_rows + offsets
    upper_half = (2 * shard_count - 1 - device_at) * half_rows + offsets
    return jnp.concatenate([lower_half, upper_half], axis=-1).reshape(-1)


def document_of(positions, doc_lengths):
    bounds = (jnp.cumsum(doc_lengths) * BLK)[:-1]
    return jnp.sum((positions[:, None] >= bounds[None, :]).astype(jnp.int32), axis=1)


def to_groups(score_matrix, shard_rows, group_width):
    grouped_heads = score_matrix.reshape(
        shard_rows, KEY_VALUE_HEADS, group_width, HEAD_SIZE
    ).transpose(1, 2, 0, 3)
    return grouped_heads.reshape(KEY_VALUE_HEADS, group_width * shard_rows, HEAD_SIZE)


def from_groups(stacked_values, shard_rows, group_width):
    spread_rows = stacked_values.reshape(
        KEY_VALUE_HEADS, group_width, shard_rows, HEAD_SIZE
    ).transpose(2, 0, 1, 3)
    return spread_rows.reshape(shard_rows, QUERY_HEAD_COUNT * HEAD_SIZE)


def local(queries, section_key_state, section_value_state, out_grad, doc_blocks):
    shard_count = lax.axis_size("ctx")
    shard_rows = queries.shape[1]
    sequence = shard_rows * shard_count
    group_width = QUERY_HEAD_COUNT // KEY_VALUE_HEADS
    piled_rows = group_width * shard_rows
    inverse_root = 1.0 / math.sqrt(HEAD_SIZE)
    block_size = min(512, sequence)
    block_count = sequence // block_size
    term_columns = 2 * KEY_VALUE_HEADS * HEAD_SIZE
    doc_lengths = doc_blocks[0]
    query_pos = layout_positions(lax.axis_index("ctx"), shard_rows, shard_count)
    key_pos = layout_positions(
        jnp.arange(shard_count, dtype=jnp.int32)[:, None], shard_rows, shard_count
    )
    query_doc = document_of(query_pos, doc_lengths)
    key_doc = document_of(key_pos, doc_lengths)
    query_groups = to_groups(queries[0], shard_rows, group_width)
    grad_groups = to_groups(out_grad[0], shard_rows, group_width)
    key_all, value_all = (
        lax.all_gather(section_key_state[0], "ctx", axis=0, tiled=True),
        lax.all_gather(section_value_state[0], "ctx", axis=0, tiled=True),
    )

    def block_inputs(first_row, total_size):
        block_pos = lax.dynamic_slice_in_dim(key_pos, first_row, total_size)
        block_doc = lax.dynamic_slice_in_dim(key_doc, first_row, total_size)
        visible = (query_doc[:, None] == block_doc[None, :]) & (
            block_pos[None, :] <= query_pos[:, None]
        )
        visible = jnp.tile(visible, (group_width, 1))[None]
        key_block = (
            lax.dynamic_slice_in_dim(key_all, first_row, total_size)
            .reshape(total_size, KEY_VALUE_HEADS, HEAD_SIZE)
            .transpose(1, 0, 2)
        )
        value_block = (
            lax.dynamic_slice_in_dim(value_all, first_row, total_size)
            .reshape(total_size, KEY_VALUE_HEADS, HEAD_SIZE)
            .transpose(1, 0, 2)
        )
        return (visible, key_block, value_block)

    def scores_of(visible, key_block):
        scores = jnp.einsum(
            "gqd,gsd->gqs", query_groups, key_block, preferred_element_type=jnp.float32
        )
        return jnp.where(visible, scores * inverse_root, -jnp.inf)

    def stat_step(block_at, carried):
        running_max, running_sum = carried
        visible, key_block, value_block = block_inputs(block_at * block_size, block_size)
        scores = scores_of(visible, key_block)
        new_max = jnp.maximum(running_max, jnp.max(scores, axis=-1))
        new_sum = running_sum * jnp.exp(running_max - new_max)
        new_sum = new_sum + jnp.sum(jnp.exp(scores - new_max[..., None]), axis=-1)
        return (new_max, new_sum)

    initial_max = jnp.full((KEY_VALUE_HEADS, piled_rows), -1e30, jnp.float32)
    initial_sum = jnp.zeros((KEY_VALUE_HEADS, piled_rows), jnp.float32)
    final_max, final_sum = lax.fori_loop(0, block_count, stat_step, (initial_max, initial_sum))
    log_total = final_max + jnp.log(final_sum)

    def out_step(block_at, accumulated):
        visible, key_block, value_block = block_inputs(block_at * block_size, block_size)
        weights_low = jnp.exp(scores_of(visible, key_block) - log_total[..., None]).astype(
            jnp.bfloat16
        )
        return accumulated + jnp.einsum(
            "gqs,gsd->gqd", weights_low, value_block, preferred_element_type=jnp.float32
        )

    blank_output = jnp.zeros((KEY_VALUE_HEADS, piled_rows, HEAD_SIZE), jnp.float32)
    out_groups = lax.fori_loop(0, block_count, out_step, blank_output).astype(jnp.bfloat16)
    row_dot = jnp.sum(grad_groups.astype(jnp.float32) * out_groups.astype(jnp.float32), axis=-1)

    def grads_of(visible, key_block, value_block):
        weights = jnp.exp(scores_of(visible, key_block) - log_total[..., None])
        weight_grad = jnp.einsum(
            "gqd,gsd->gqs", grad_groups, value_block, preferred_element_type=jnp.float32
        )
        score_grad = (weights * (weight_grad - row_dot[..., None]) * inverse_root).astype(
            jnp.bfloat16
        )
        return (weights.astype(jnp.bfloat16), score_grad)

    def key_terms(weights_low, score_grad, total_size):
        key_term = jnp.einsum(
            "gqs,gqd->sgd", score_grad, query_groups, preferred_element_type=jnp.float32
        ).reshape(total_size, KEY_VALUE_HEADS * HEAD_SIZE)
        value_term = jnp.einsum(
            "gqs,gqd->sgd", weights_low, grad_groups, preferred_element_type=jnp.float32
        ).reshape(total_size, KEY_VALUE_HEADS * HEAD_SIZE)
        return jnp.concatenate([key_term, value_term], axis=-1)

    def back_step(query_grad, block_at):
        visible, key_block, value_block = block_inputs(block_at * block_size, block_size)
        weights_low, score_grad = grads_of(visible, key_block, value_block)
        new_grad = query_grad + jnp.einsum(
            "gqs,gsd->gqd", score_grad, key_block, preferred_element_type=jnp.float32
        )
        return (new_grad, key_terms(weights_low, score_grad, block_size))

    blank_gradient = jnp.zeros((KEY_VALUE_HEADS, piled_rows, HEAD_SIZE), jnp.float32)
    query_grad, block_terms = lax.scan(
        back_step, blank_gradient, jnp.arange(block_count, dtype=jnp.int32)
    )
    query_rows = from_groups(query_grad.astype(jnp.bfloat16), shard_rows, group_width)
    pair_sum = lax.psum_scatter(
        block_terms.reshape(sequence, term_columns).astype(jnp.bfloat16),
        "ctx",
        scatter_dimension=0,
        tiled=True,
    )
    joined = jnp.concatenate([query_rows, pair_sum], axis=-1)[None]
    sent_back = from_behind(joined, "pipe", -1)
    query_sent = sent_back[:, :, : QUERY_HEAD_COUNT * HEAD_SIZE]
    pair_passed = sent_back[:, :, QUERY_HEAD_COUNT * HEAD_SIZE :]
    attention = from_groups(out_groups, shard_rows, group_width)[None]
    key_passed = pair_passed[:, :, : KEY_VALUE_HEADS * HEAD_SIZE]
    value_passed = pair_passed[:, :, KEY_VALUE_HEADS * HEAD_SIZE :]
    return (attention, query_sent, key_passed, value_passed)


def solution(mesh):
    return jax.shard_map(
        local,
        mesh=mesh,
        in_specs=(
            P(("dp", "pipe"), "ctx", None),
            P(("dp", "pipe"), "ctx", None),
            P(("dp", "pipe"), "ctx", None),
            P(("dp", "pipe"), "ctx", None),
            P(("dp", "pipe"), None),
        ),
        out_specs=(
            P(("dp", "pipe"), "ctx", None),
            P(("dp", "pipe"), "ctx", None),
            P(("dp", "pipe"), "ctx", None),
            P(("dp", "pipe"), "ctx", None),
        ),
        check_vma=False,
    )
```

profile of v0, /device:TPU:0, one launch (start us, length us, event | category | flops | bytes accessed | tf_op | source)
XLA Modules:
  0.0 227.1 jit_solution(4679452469479922389)
XLA Ops:
  7.3 0.8 reduce-window.9
  8.5 1.1 copy.93
  9.7 0.6 copy.75
  10.9 29.5 %all-gather = bf16[1,1024,256]{1,2,0:T(8,128)(2,1)S(1)} all-gather(bf16[1,128,256]{1,2,0:T(8,128)(2,1)S(1)} %copy.74), channel_id=2, replica_groups=mesh['dp'=2,'pipe'=2,'ctx'=8] {'ctx'}, dimensions={1}, use_global_device_ids=true | all-gather | bytes 589824 | tf_op jit(solution)/shard_map/all_gather | solution.py:66
  40.5 14.3 %while.43 = (s32[]{:T(128)}, f32[2,1024]{1,0:T(2,128)S(1)}, f32[2,1024]{1,0:T(2,128)S(1)}, s32[128]{0:T(128)S(1)}, s32[1024]{0:T(1024)S(1)}, /*index=5*/s32[1024...) while((s32[]{:T(128)}, f32[2,1024]{1,0:T(2,128)S(1)}, ...), condition=%wide.region_6.7_spmd.clone, body=%wide.region_3.6_spmd.clone.sunk | while | flops 275982336 | bytes 13096130 | solution.py:106
  41.6 2.8 %fusion.64 = (f32[2,1024]{1,0:T(2,128)S(1)}, f32[2,512,1024]{2,1,0:T(8,128)}) fusion(pred[1024,512]{0,1:T(8,128)(4,1)S(1)} %bitcast.211, bf16[2,1024,128]{2,1,0:T(8,128)(2,1)S(1)} %get-tuple-element.915, bf16[512,2,128]{2,0,1:T(8,128)(2,1)S(1)} %copy.114), kind=kOutput, calls=%fused_computation.2.clone.1 | convolution fusion | flops 271579136 | bytes 5513216 | tf_op jit(solution)/shard_map/while/body/eval_jaxpr/gqd,gsd->gqs/dot_general | solution.py:90
  44.4 3.2 %exponential_reduce_fusion.2 = f32[2,1024]{1,0:T(2,128)S(1)} fusion(f32[2,512,1024]{2,1,0:T(8,128)} %get-tuple-element.852, f32[2,1024]{1,0:T(2,128)S(1)} %fusion.65, pred[1024,512]{0,1:T(8,128)(4,1)S(1)} %bitcast.212), kind=kLoop, calls=%fused_computation.1.clone.1 | loop fusion | flops 4192256 | bytes 4734976 | tf_op jit(solution)/shard_map/while/body/eval_jaxpr/reduce_sum | solution.py:101
  48.7 2.8 %fusion.64 = (f32[2,1024]{1,0:T(2,128)S(1)}, f32[2,512,1024]{2,1,0:T(8,128)}) fusion(pred[1024,512]{0,1:T(8,128)(4,1)S(1)} %bitcast.211, bf16[2,1024,128]{2,1,0:T(8,128)(2,1)S(1)} %get-tuple-element.915, bf16[512,2,128]{2,0,1:T(8,128)(2,1)S(1)} %copy.114), kind=kOutput, calls=%fused_computation.2.clone.1 | convolution fusion | flops 271579136 | bytes 5513216 | tf_op jit(solution)/shard_map/while/body/eval_jaxpr/gqd,gsd->gqs/dot_general | solution.py:90
  51.6 3.2 %exponential_reduce_fusion.2 = f32[2,1024]{1,0:T(2,128)S(1)} fusion(f32[2,512,1024]{2,1,0:T(8,128)} %get-tuple-element.852, f32[2,1024]{1,0:T(2,128)S(1)} %fusion.65, pred[1024,512]{0,1:T(8,128)(4,1)S(1)} %bitcast.212), kind=kLoop, calls=%fused_computation.1.clone.1 | loop fusion | flops 4192256 | bytes 4734976 | tf_op jit(solution)/shard_map/while/body/eval_jaxpr/reduce_sum | solution.py:101
  54.9 28.8 %all-gather.1 = bf16[1,1024,256]{1,2,0:T(8,128)(2,1)} all-gather(bf16[1,128,256]{1,2,0:T(8,128)(2,1)S(1)} %copy.77), channel_id=3, replica_groups=mesh['dp'=2,'pipe'=2,'ctx'=8] {'ctx'}, dimensions={1}, use_global_device_ids=true | all-gather | bytes 589824 | tf_op jit(solution)/shard_map/all_gather | solution.py:67
  83.8 11.5 %while.44 = (s32[]{:T(128)}, f32[2,1024,128]{2,1,0:T(8,128)}, s32[128]{0:T(128)S(1)}, s32[1024]{0:T(1024)S(1)}, s32[1024]{0:T(1024)S(1)}, /*index=5*/s32[128]{0:...) while((s32[]{:T(128)}, f32[2,1024,128]{2,1,0:T(8,128)}, ...), condition=%wide.region_8.9_spmd.clone, body=%wide.region_7.8_spmd.clone.sunk | while | flops 541786112 | bytes 7492809 | solution.py:119
  84.6 1.0 constant_dynamic-slice_fusion.9
  86.0 2.9 %fusion.70 = f32[2,1024,128]{2,1,0:T(8,128)} fusion(bf16[2,1024,128]{2,1,0:T(8,128)(2,1)S(1)} %get-tuple-element.955, f32[2,1024]{1,0:T(2,128)S(1)} %get-tuple-element.956, pred[1024,512]{0,1:T(8,128)(4,1)S(1)} %bitcast.225, f32[2,1024,128]{2,1,0:T(8,128)} %get-tuple-element.935, pred[]{:T(512)S(6)} %compare.10, ...), kind=kOutput, calls=%fused_computation.18.clone.1 | convolution fusion | flops 541589504 | bytes 3678209 | tf_op jit(solution)/shard_map/while/body/eval_jaxpr/gqs,gsd->gqd/dot_general | solution.py:114
  89.8 1.0 constant_dynamic-slice_fusion.9
  91.1 4.1 %fusion.70 = f32[2,1024,128]{2,1,0:T(8,128)} fusion(bf16[2,1024,128]{2,1,0:T(8,128)(2,1)S(1)} %get-tuple-element.955, f32[2,1024]{1,0:T(2,128)S(1)} %get-tuple-element.956, pred[1024,512]{0,1:T(8,128)(4,1)S(1)} %bitcast.225, f32[2,1024,128]{2,1,0:T(8,128)} %get-tuple-element.935, pred[]{:T(512)S(6)} %compare.10, ...), kind=kOutput, calls=%fused_computation.18.clone.1 | convolution fusion | flops 541589504 | bytes 3678209 | tf_op jit(solution)/shard_map/while/body/eval_jaxpr/gqs,gsd->gqd/dot_general | solution.py:114
  95.2 1.4 copy.79
  96.8 0.6 copy.81
  97.4 1.0 reshape.296
  98.4 1.2 multiply_reduce_fusion
  99.7 37.0 %while.45 = (s32[]{:T(128)}, f32[2,1024,128]{2,1,0:T(8,128)}, bf16[2,512,512]{1,2,0:T(8,128)(2,1)}, s32[128]{0:T(128)S(1)}, s32[2]{0:T(128)S(1)}, /*index=5*/s32...) while((s32[]{:T(128)}, f32[2,1024,128]{2,1,0:T(8,128)}, ...), condition=%wide.region_11.12_spmd.clone, body=%wide.region_10.11_spmd.clone.sunk | while | flops 1355481088 | bytes 49190700 | solution.py:150
  99.7 0.6 dynamic_slice.99
  101.6 1.1 copy.119
  102.6 1.0 constant_dynamic-slice_fusion.10
  103.8 2.6 %fusion.81 = f32[2,512,1024]{2,1,0:T(8,128)} fusion(bf16[2,1024,128]{1,2,0:T(8,128)(2,1)S(1)} %get-tuple-element.1007, bf16[512,2,128]{2,0,1:T(8,128)(2,1)S(1)} %copy.118), kind=kOutput, calls=%fused_computation.41.clone.1 | convolution fusion | flops 268435456 | bytes 4980736 | tf_op jit(solution)/shard_map/while/body/eval_jaxpr/gqd,gsd->gqs/dot_general | solution.py:90
  106.4 0.9 copy.120
  107.3 4.3 %fusion.82 = bf16[2,1024,512]{1,2,0:T(8,128)(2,1)S(1)} fusion(f32[2,512,1024]{2,1,0:T(8,128)} %fusion.81, bf16[2,1024,128]{1,2,0:T(8,128)(2,1)} %get-tuple-element.1010, f32[2,1024]{1,0:T(2,128)S(1)} %get-tuple-element.1011, f32[2,1024]{1,0:T(2,128)S(1)} %get-tuple-element.1008, pred[1024,512]{0,1:T(8,128)(4,1)} %bitcast.223, ...), kind=kOutput, calls=%fused_computation.28.clone.1 | convolution fusion | flops 275775488 | bytes 7618560 | tf_op jit(solution)/shard_map/while/body/eval_jaxpr/gqd,gsd->gqs/dot_general | solution.py:124
  111.6 0.8 fusion.84
  112.5 2.4 %fusion.83 = bf16[2,512,128]{1,2,0:T(8,128)(2,1)S(1)} fusion(bf16[2,1024,128]{1,2,0:T(8,128)(2,1)} %get-tuple-element.1010, f32[2,512,1024]{2,1,0:T(8,128)S(1)} %copy-done, f32[2,1024]{1,0:T(2,128)S(1)} %get-tuple-element.1008, pred[1024,512]{0,1:T(8,128)(4,1)S(1)} %bitcast.224), kind=kOutput, calls=%fused_computation.33.clone.1 | convolution fusion | flops 272629760 | bytes 5513216 | tf_op jit(solution)/shard_map/while/body/eval_jaxpr/gqs,gqd->sgd/dot_general | solution.py:136
  114.8 0.8 fusion.85
  115.7 1.9 convolution_add_fusion.2
  119.4 1.1 copy.119
  120.5 1.0 constant_dynamic-slice_fusion.10
  121.7 2.6 %fusion.81 = f32[2,512,1024]{2,1,0:T(8,128)} fusion(bf16[2,1024,128]{1,2,0:T(8,128)(2,1)S(1)} %get-tuple-element.1007, bf16[512,2,128]{2,0,1:T(8,128)(2,1)S(1)} %copy.118), kind=kOutput, calls=%fused_computation.41.clone.1 | convolution fusion | flops 268435456 | bytes 4980736 | tf_op jit(solution)/shard_map/while/body/eval_jaxpr/gqd,gsd->gqs/dot_general | solution.py:90
  124.3 0.9 copy.120
  125.2 4.3 %fusion.82 = bf16[2,1024,512]{1,2,0:T(8,128)(2,1)S(1)} fusion(f32[2,512,1024]{2,1,0:T(8,128)} %fusion.81, bf16[2,1024,128]{1,2,0:T(8,128)(2,1)} %get-tuple-element.1010, f32[2,1024]{1,0:T(2,128)S(1)} %get-tuple-element.1011, f32[2,1024]{1,0:T(2,128)S(1)} %get-tuple-element.1008, pred[1024,512]{0,1:T(8,128)(4,1)} %bitcast.223, ...), kind=kOutput, calls=%fused_computation.28.clone.1 | convolution fusion | flops 275775488 | bytes 7618560 | tf_op jit(solution)/shard_map/while/body/eval_jaxpr/gqd,gsd->gqs/dot_general | solution.py:124
  129.5 0.8 fusion.84
  130.3 2.4 %fusion.83 = bf16[2,512,128]{1,2,0:T(8,128)(2,1)S(1)} fusion(bf16[2,1024,128]{1,2,0:T(8,128)(2,1)} %get-tuple-element.1010, f32[2,512,1024]{2,1,0:T(8,128)S(1)} %copy-done, f32[2,1024]{1,0:T(2,128)S(1)} %get-tuple-element.1008, pred[1024,512]{0,1:T(8,128)(4,1)S(1)} %bitcast.224), kind=kOutput, calls=%fused_computation.33.clone.1 | convolution fusion | flops 272629760 | bytes 5513216 | tf_op jit(solution)/shard_map/while/body/eval_jaxpr/gqs,gqd->sgd/dot_general | solution.py:136
  132.7 0.8 fusion.85
  133.5 3.1 %convolution_add_fusion.2 = f32[2,1024,128]{2,1,0:T(8,128)} fusion(bf16[2,1024,512]{1,2,0:T(8,128)(2,1)S(1)} %fusion.82, f32[2,1024,128]{2,1,0:T(8,128)} %get-tuple-element.981, pred[]{:T(512)S(6)} %compare.11, bf16[512,2,128]{2,0,1:T(8,128)(2,1)S(1)} %copy.118), kind=kOutput, calls=%fused_computation.36.clone.1 | convolution fusion | flops 268959744 | bytes 4456449 | tf_op jit(solution)/shard_map/while/body/eval_jaxpr/gqs,gsd->gqd/dot_general | solution.py:144
  136.7 2.3 %copy.83 = bf16[2,512,512]{2,1,0:T(8,128)(2,1)} copy(bf16[2,512,512]{1,2,0:T(8,128)(2,1)} %get-tuple-element.405) | data formatting | bytes 2097152 | tf_op jit(solution)/shard_map/convert_element_type | solution.py:155
  139.1 1.3 convert_element_type.42
  140.8 60.1 %reduce-scatter.2.cloned.1.call-done = bf16[128,512]{1,0:T(8,128)(2,1)} async-done(((bf16[1024,512]{1,0:T(8,128)(2,1)}), bf16[128,512]{1,0:T(8,128)(2,1)}) %reduce-scatter.2.cloned.1.call-update) | async-done | bytes 131088 | tf_op jit(solution)/shard_map/reduce_scatter | solution.py:154
  201.0 0.9 maximum_bitcast_fusion.1
  201.9 1.3 collective-permute-start
  203.9 1.0 broadcast_in_dim_reshape.4
  205.0 13.8 %collective-permute-done = bf16[1,128,2560]{2,1,0:T(8,128)(2,1)S(1)} collective-permute-done((bf16[1,128,2560]{2,1,0:T(8,128)(2,1)S(1)}, bf16[1,128,2560]{2,1,0:T(8,128)(2,1)S(1)}, u32[]{:S(2)}, u32[]{:S(2)}) %collective-permute-start) | collective-permute-done | bytes 655392 | tf_op jit(solution)/shard_map/ppermute | solution.py:16
  218.8 0.8 slice.24
  219.6 0.7 fusion.30
  (91 shorter events, 9.2 us)
Async XLA Ops:
  7.2 3.6 %copy-start.5 = (bf16[1,128,256]{2,1,0:T(8,128)(2,1)S(1)}, bf16[1,128,256]{2,1,0:T(8,128)(2,1)}, u32[]{:S(2)}) copy-start(bf16[1,128,256]{2,1,0:T(8,128)(2,1)} %param.12) | copy-start | bytes 196612
  7.2 193.8 %reduce-scatter.2.cloned.1.call-start = ((), (), s32[]{:S(2)}) async-start(), calls=%async_computation.1 | async-start | bytes 1179648 | tf_op jit(solution)/shard_map/reduce_scatter | solution.py:154
  40.5 14.3 %copy-start.6 = (bf16[1,128,256]{2,1,0:T(8,128)(2,1)S(1)}, bf16[1,128,256]{2,1,0:T(8,128)(2,1)}, u32[]{:S(2)}) copy-start(bf16[1,128,256]{2,1,0:T(8,128)(2,1)} %param.13) | copy-start | bytes 196612
  83.7 13.0 %copy-start.4 = (bf16[1,128,2048]{2,1,0:T(8,128)(2,1)S(1)}, bf16[1,128,2048]{2,1,0:T(8,128)(2,1)}, u32[]{:S(2)}) copy-start(bf16[1,128,2048]{2,1,0:T(8,128)(2,1)} %param.14) | copy-start | bytes 1572868
  96.7 3.0 %copy-start.2 = (bf16[2,1024,128]{1,2,0:T(8,128)(2,1)}, bf16[2,1024,128]{1,2,0:T(8,128)(2,1)S(1)}, u32[]{:S(2)}) copy-start(bf16[2,1024,128]{1,2,0:T(8,128)(2,1)S(1)} %copy.79) | copy-start | bytes 1572868
  107.3 5.2 %copy-start = (f32[2,512,1024]{2,1,0:T(8,128)S(1)}, f32[2,512,1024]{2,1,0:T(8,128)}, u32[]{:S(2)}) copy-start(f32[2,512,1024]{2,1,0:T(8,128)} %fusion.81) | copy-start | bytes 12582916 | tf_op jit(solution)/shard_map/while
  107.3 5.2 %copy-start.1 = (pred[64,8,8,128]{3,1,2,0:T(8,128)(4,1)S(1)}, pred[64,8,8,128]{3,1,2,0:T(8,128)(4,1)}, u32[]{:S(2)}) copy-start(pred[64,8,8,128]{3,1,2,0:T(8,128)(4,1)} %copy.119) | copy-start | bytes 1572868 | tf_op jit(solution)/shard_map/while
  125.1 5.2 %copy-start = (f32[2,512,1024]{2,1,0:T(8,128)S(1)}, f32[2,512,1024]{2,1,0:T(8,128)}, u32[]{:S(2)}) copy-start(f32[2,512,1024]{2,1,0:T(8,128)} %fusion.81) | copy-start | bytes 12582916 | tf_op jit(solution)/shard_map/while
  125.1 5.2 %copy-start.1 = (pred[64,8,8,128]{3,1,2,0:T(8,128)(4,1)S(1)}, pred[64,8,8,128]{3,1,2,0:T(8,128)(4,1)}, u32[]{:S(2)}) copy-start(pred[64,8,8,128]{3,1,2,0:T(8,128)(4,1)} %copy.119) | copy-start | bytes 1572868 | tf_op jit(solution)/shard_map/while
  136.7 66.6 %copy-start.3 = (bf16[2,1024,128]{1,2,0:T(8,128)(2,1)S(1)}, bf16[2,1024,128]{1,2,0:T(8,128)(2,1)}, u32[]{:S(2)}) copy-start(bf16[2,1024,128]{1,2,0:T(8,128)(2,1)} %copy-done.2) | copy-start | bytes 1572868
  201.9 16.8 %collective-permute-start = (bf16[1,128,2560]{2,1,0:T(8,128)(2,1)S(1)}, bf16[1,128,2560]{2,1,0:T(8,128)(2,1)S(1)}, u32[]{:S(2)}, u32[]{:S(2)}) collective-permute-start(bf16[1,128,2560]{2,1,0:T(8,128)(2,1)S(1)} %maximum_bitcast_fusion.1), channel_id=1, source_target_pairs={{8,0},{9,1},{10,2},{11,3},{12,4},{13,5},{14,6},{15,7},{24,16},{25,... | collective-permute-start | bytes 1966088 | tf_op jit(solution)/shard_map/ppermute | solution.py:16
Sparse Core Ops, SparseCore 0:
  139.2 61.7 reduce-scatter.1
where the time goes:
time: 228 us; the launch traced here: 227 us
  waiting for transfers between devices  74 us (32%)
  blocking collectives  58.3 us (26%)
  matrix products  38 us (17%)
  local copies, waits for them, and re-layouts  25.5 us (11%)
  between operations  14.3 us (6%)
  other arithmetic  14 us (6%)
    reduce_scatter x1, waiting for transfers between devices, local(): lax.psum_scatter(block_terms.reshape(sequence, term_columns).astype(jnp.b...  60.1 us
    all_gather x1, blocking collectives, local(): lax.all_gather(section_key_state[0], 'ctx', axis=0, tiled=True)  29.5 us
    all_gather x1, blocking collectives, local(): lax.all_gather(section_value_state[0], 'ctx', axis=0, tiled=True)  28.8 us
    ppermute x1, waiting for transfers between devices, from_behind(): return lax.ppermute(x, axis, pairs)  13.8 us
    dot_general x4, matrix products, scores_of(): jnp.einsum('gqd,gsd->gqs', query_groups, key_block, preferred_element_typ...  11 us
    dot_general x2, matrix products, grads_of(): jnp.einsum('gqd,gsd->gqs', grad_groups, value_block, preferred_element_ty...  8.62 us
    dot_general x2, matrix products, out_step(): jnp.einsum('gqs,gsd->gqd', weights_low, value_block, preferred_element_ty...  6.99 us
    reduce_sum x2, other arithmetic, stat_step(): new_sum = new_sum + jnp.sum(jnp.exp(scores - new_max[..., None]), axis=-1)  6.32 us
  transfers between devices with their start and end apart: 2, of which 2 were waited for; matrix products, arithmetic and copies ran while one was open for 2% of the time, Pallas kernels for 0%

commit v1 on v0

--- a/solution.py
+++ b/solution.py
@@ -8,6 +8,24 @@
 KEY_VALUE_HEADS = 2
 HEAD_SIZE = 128
 BLK = 128
+
+
+def order_the_indices(v0, dim_k):
+    formed = list(v0.shape[1:])
+    formed[dim_k] *= v0.shape[0]
+    return jnp.moveaxis(v0, 0, dim_k).reshape(formed)
+
+
+def goods_review(target, device_axis):
+    n_slots = lax.axis_size(device_axis)
+    top = target[None]
+    for at in range(n_slots.bit_length() - 1):
+        heard = 1 << at
+        prior = lax.ppermute(top, device_axis, [(dd, dd ^ heard) for dd in range(n_slots)])
+        r2 = jnp.stack([top, prior])
+        step_out = lax.axis_index(device_axis) >> at & 1
+        top = jnp.where(step_out == 0, r2, r2[::-1]).reshape(-1, *target.shape)
+    return top
 
 
 def from_behind(x, axis, by):
@@ -44,6 +62,10 @@
 
 
 def local(queries, section_key_state, section_value_state, out_grad, doc_blocks):
+
+    def replace_the_chains(base_x, inp, array_dim):
+        return order_the_indices(goods_review(base_x, inp), array_dim)
+
     shard_count = lax.axis_size("ctx")
     shard_rows = queries.shape[1]
     sequence = shard_rows * shard_count
@@ -64,7 +86,7 @@
     grad_groups = to_groups(out_grad[0], shard_rows, group_width)
     key_all, value_all = (
         lax.all_gather(section_key_state[0], "ctx", axis=0, tiled=True),
-        lax.all_gather(section_value_state[0], "ctx", axis=0, tiled=True),
+        replace_the_chains(section_value_state[0], "ctx", 0),
     )
 
     def block_inputs(first_row, total_size):

time: 228 us -> 212 us (0.930)
  blocking collectives: 58.3 us -> 27.9 us
  starting transfers between devices: 1.33 us -> 5.98 us
  waiting for transfers between devices: 74 us -> 77.6 us
  other arithmetic: 14 us -> 16.8 us
  local copies, waits for them, and re-layouts: 25.5 us -> 28.3 us
    all_gather x1 -> x0, blocking collectives: 28.8 us -> none  [local(): lax.all_gather(section_value_state[0], 'ctx', axis=0, tiled=True)]
    ppermute x0 -> x3, starting transfers between devices: none -> 4.65 us  [goods_review(): lax.ppermute(top, device_axis, [(dd, dd ^ heard) for dd in range(n_slots)])]
    ppermute x0 -> x3, waiting for transfers between devices: none -> 2.93 us  [goods_review(): lax.ppermute(top, device_axis, [(dd, dd ^ heard) for dd in range(n_slots)])]
  transfers between devices with their start and end apart: 2 -> 5, of which waited for: 2 -> 3; matrix products, arithmetic and copies ran while one was open for 2% -> 11% of each run, Pallas kernels for 0% -> 0%
where the time goes in v1:
time: 212 us; the launch traced here: 211 us
  waiting for transfers between devices  77.6 us (37%)
  matrix products  37.9 us (18%)
  local copies, waits for them, and re-layouts  28.3 us (13%)
  blocking collectives  27.9 us (13%)
  other arithmetic  16.8 us (8%)
  between operations  14.3 us (7%)
  starting transfers between devices  5.98 us (3%)
    reduce_scatter x1, waiting for transfers between devices, local(): lax.psum_scatter(block_terms.reshape(sequence, term_columns).astype(jnp.b...  60.9 us
    all_gather x1, blocking collectives, local(): lax.all_gather(section_key_state[0], 'ctx', axis=0, tiled=True)  27.9 us
    ppermute x1, waiting for transfers between devices, from_behind(): return lax.ppermute(x, axis, pairs)  13.8 us
    dot_general x4, matrix products, scores_of(): jnp.einsum('gqd,gsd->gqs', query_groups, key_block, preferred_element_typ...  11 us
    dot_general x2, matrix products, grads_of(): jnp.einsum('gqd,gsd->gqs', grad_groups, value_block, preferred_element_ty...  8.63 us
    dot_general x2, matrix products, out_step(): jnp.einsum('gqs,gsd->gqd', weights_low, value_block, preferred_element_ty...  6.91 us
    reduce_sum x2, other arithmetic, stat_step(): new_sum = new_sum + jnp.sum(jnp.exp(scores - new_max[..., None]), axis=-1)  6.32 us
    dot_general x2, matrix products, back_step(): jnp.einsum('gqs,gsd->gqd', score_grad, key_block, preferred_element_type=...  5.03 us
  transfers between devices with their start and end apart: 5, of which 3 were waited for; matrix products, arithmetic and copies ran while one was open for 11% of the time, Pallas kernels for 0%

profile of v1, /device:TPU:0, one launch (start us, length us, event | category | flops | bytes accessed | tf_op | source)
XLA Modules:
  0.0 210.7 jit_solution(2678711700474840828)
XLA Ops:
  7.2 3.0 %collective-permute-start = (bf16[1,128,256]{2,1,0:T(8,128)(2,1)}, bf16[1,128,256]{2,1,0:T(8,128)(2,1)S(1)}, u32[]{:S(2)}, u32[]{:S(2)}) collective-permute-start(bf16[1,128,256]{2,1,0:T(8,128)(2,1)} %param.13), channel_id=1, source_target_pairs={{0,1},{1,0},{2,3},{3,2},{4,5},{5,4},{6,7},{7,6},{8,9},{9,8},{10,11... | collective-permute-start | bytes 196616 | tf_op jit(solution)/shard_map/ppermute | solution.py:24
  11.1 0.9 copy.76
  12.0 27.9 %all-gather = bf16[1,1024,256]{1,2,0:T(8,128)(2,1)S(1)} all-gather(bf16[1,128,256]{1,2,0:T(8,128)(2,1)S(1)} %copy.76), channel_id=2, replica_groups=mesh['dp'=2,'pipe'=2,'ctx'=8] {'ctx'}, dimensions={1}, use_global_device_ids=true | all-gather | bytes 589824 | tf_op jit(solution)/shard_map/all_gather | solution.py:88
  40.2 0.9 pad_maximum_fusion.2
  41.9 1.1 copy.96
  44.3 2.9 %collective-permute-done.1 = bf16[2,128,256]{2,1,0:T(8,128)(2,1)S(1)} collective-permute-done((bf16[2,128,256]{2,1,0:T(8,128)(2,1)S(1)}, bf16[2,128,256]{2,1,0:T(8,128)(2,1)S(1)}, u32[]{:S(2)}, u32[]{:S(2)}) %collective-permute-start.1) | collective-permute-done | bytes 131104 | tf_op jit(solution)/shard_map/ppermute | solution.py:24
  47.3 0.9 copy.79
  48.2 0.9 collective-permute-start.2
  49.0 14.3 %while.43 = (s32[]{:T(128)}, f32[2,1024]{1,0:T(2,128)S(1)}, f32[2,1024]{1,0:T(2,128)S(1)}, s32[128]{0:T(128)S(1)}, s32[1024]{0:T(1024)S(1)}, /*index=5*/s32[1024...) while((s32[]{:T(128)}, f32[2,1024]{1,0:T(2,128)S(1)}, ...), condition=%wide.region_6.7_spmd.clone, body=%wide.region_3.6_spmd.clone.sunk | while | flops 275982336 | bytes 13096130 | solution.py:128
  50.1 2.9 %fusion.66 = (f32[2,1024]{1,0:T(2,128)S(1)}, f32[2,512,1024]{2,1,0:T(8,128)}) fusion(pred[1024,512]{0,1:T(8,128)(4,1)S(1)} %bitcast.222, bf16[2,1024,128]{2,1,0:T(8,128)(2,1)S(1)} %get-tuple-element.917, bf16[512,2,128]{2,0,1:T(8,128)(2,1)S(1)} %copy.117), kind=kOutput, calls=%fused_computation.2.clone.1 | convolution fusion | flops 271579136 | bytes 5513216 | tf_op jit(solution)/shard_map/while/body/eval_jaxpr/gqd,gsd->gqs/dot_general | solution.py:112
  53.0 3.2 %exponential_reduce_fusion.2 = f32[2,1024]{1,0:T(2,128)S(1)} fusion(f32[2,512,1024]{2,1,0:T(8,128)} %get-tuple-element.854, f32[2,1024]{1,0:T(2,128)S(1)} %fusion.67, pred[1024,512]{0,1:T(8,128)(4,1)S(1)} %bitcast.223), kind=kLoop, calls=%fused_computation.1.clone.1 | loop fusion | flops 4192256 | bytes 4734976 | tf_op jit(solution)/shard_map/while/body/eval_jaxpr/reduce_sum | solution.py:123
  57.3 2.9 %fusion.66 = (f32[2,1024]{1,0:T(2,128)S(1)}, f32[2,512,1024]{2,1,0:T(8,128)}) fusion(pred[1024,512]{0,1:T(8,128)(4,1)S(1)} %bitcast.222, bf16[2,1024,128]{2,1,0:T(8,128)(2,1)S(1)} %get-tuple-element.917, bf16[512,2,128]{2,0,1:T(8,128)(2,1)S(1)} %copy.117), kind=kOutput, calls=%fused_computation.2.clone.1 | convolution fusion | flops 271579136 | bytes 5513216 | tf_op jit(solution)/shard_map/while/body/eval_jaxpr/gqd,gsd->gqs/dot_general | solution.py:112
  60.1 3.2 %exponential_reduce_fusion.2 = f32[2,1024]{1,0:T(2,128)S(1)} fusion(f32[2,512,1024]{2,1,0:T(8,128)} %get-tuple-element.854, f32[2,1024]{1,0:T(2,128)S(1)} %fusion.67, pred[1024,512]{0,1:T(8,128)(4,1)S(1)} %bitcast.223), kind=kLoop, calls=%fused_computation.1.clone.1 | loop fusion | flops 4192256 | bytes 4734976 | tf_op jit(solution)/shard_map/while/body/eval_jaxpr/reduce_sum | solution.py:123
  64.1 1.0 reshape.304
  65.4 1.3 pad_maximum_fusion
  67.0 1.2 reshape_reshape.3
  68.1 11.4 %while.44 = (s32[]{:T(128)}, f32[2,1024,128]{2,1,0:T(8,128)}, s32[128]{0:T(128)S(1)}, s32[1024]{0:T(1024)S(1)}, s32[1024]{0:T(1024)S(1)}, /*index=5*/s32[128]{0:...) while((s32[]{:T(128)}, f32[2,1024,128]{2,1,0:T(8,128)}, ...), condition=%wide.region_8.9_spmd.clone, body=%wide.region_7.8_spmd.clone.sunk | while | flops 541786112 | bytes 7492809 | solution.py:141
  69.0 1.0 constant_dynamic-slice_fusion.9
  70.4 2.8 %fusion.72 = f32[2,1024,128]{2,1,0:T(8,128)} fusion(bf16[2,1024,128]{2,1,0:T(8,128)(2,1)S(1)} %get-tuple-element.957, f32[2,1024]{1,0:T(2,128)S(1)} %get-tuple-element.958, pred[1024,512]{0,1:T(8,128)(4,1)S(1)} %bitcast.236, f32[2,1024,128]{2,1,0:T(8,128)} %get-tuple-element.937, pred[]{:T(512)S(6)} %compare.10, ...), kind=kOutput, calls=%fused_computation.18.clone.1 | convolution fusion | flops 541589504 | bytes 3678209 | tf_op jit(solution)/shard_map/while/body/eval_jaxpr/gqs,gsd->gqd/dot_general | solution.py:136
  74.1 1.0 constant_dynamic-slice_fusion.9
  75.4 4.1 %fusion.72 = f32[2,1024,128]{2,1,0:T(8,128)} fusion(bf16[2,1024,128]{2,1,0:T(8,128)(2,1)S(1)} %get-tuple-element.957, f32[2,1024]{1,0:T(2,128)S(1)} %get-tuple-element.958, pred[1024,512]{0,1:T(8,128)(4,1)S(1)} %bitcast.236, f32[2,1024,128]{2,1,0:T(8,128)} %get-tuple-element.937, pred[]{:T(512)S(6)} %compare.10, ...), kind=kOutput, calls=%fused_computation.18.clone.1 | convolution fusion | flops 541589504 | bytes 3678209 | tf_op jit(solution)/shard_map/while/body/eval_jaxpr/gqs,gsd->gqd/dot_general | solution.py:136
  79.5 1.4 copy.82
  81.0 1.4 multiply_reduce_fusion
  82.4 37.1 %while.45 = (s32[]{:T(128)}, f32[2,1024,128]{2,1,0:T(8,128)}, bf16[2,512,512]{1,2,0:T(8,128)(2,1)}, s32[128]{0:T(128)S(1)}, s32[2]{0:T(128)S(1)}, /*index=5*/s32...) while((s32[]{:T(128)}, f32[2,1024,128]{2,1,0:T(8,128)}, ...), condition=%wide.region_11.12_spmd.clone, body=%wide.region_10.11_spmd.clone.sunk | while | flops 1355481088 | bytes 49190700 | solution.py:172
  84.4 1.1 copy.122
  85.5 1.0 constant_dynamic-slice_fusion.10
  86.7 2.6 %fusion.83 = f32[2,512,1024]{2,1,0:T(8,128)} fusion(bf16[2,1024,128]{1,2,0:T(8,128)(2,1)S(1)} %get-tuple-element.1009, bf16[512,2,128]{2,0,1:T(8,128)(2,1)S(1)} %copy.121), kind=kOutput, calls=%fused_computation.41.clone.1 | convolution fusion | flops 268435456 | bytes 4980736 | tf_op jit(solution)/shard_map/while/body/eval_jaxpr/gqd,gsd->gqs/dot_general | solution.py:112
  90.2 4.3 %fusion.84 = bf16[2,1024,512]{1,2,0:T(8,128)(2,1)S(1)} fusion(f32[2,512,1024]{2,1,0:T(8,128)} %fusion.83, bf16[2,1024,128]{1,2,0:T(8,128)(2,1)} %get-tuple-element.1012, f32[2,1024]{1,0:T(2,128)S(1)} %get-tuple-element.1013, f32[2,1024]{1,0:T(2,128)S(1)} %get-tuple-element.1010, pred[1024,512]{0,1:T(8,128)(4,1)} %bitcast.234, ...), kind=kOutput, calls=%fused_computation.28.clone.1 | convolution fusion | flops 275775488 | bytes 7618560 | tf_op jit(solution)/shard_map/while/body/eval_jaxpr/gqd,gsd->gqs/dot_general | solution.py:146
  94.5 0.8 fusion.86
  95.3 2.3 %fusion.85 = bf16[2,512,128]{1,2,0:T(8,128)(2,1)S(1)} fusion(bf16[2,1024,128]{1,2,0:T(8,128)(2,1)} %get-tuple-element.1012, f32[2,512,1024]{2,1,0:T(8,128)S(1)} %copy-done, f32[2,1024]{1,0:T(2,128)S(1)} %get-tuple-element.1010, pred[1024,512]{0,1:T(8,128)(4,1)S(1)} %bitcast.235), kind=kOutput, calls=%fused_computation.33.clone.1 | convolution fusion | flops 272629760 | bytes 5513216 | tf_op jit(solution)/shard_map/while/body/eval_jaxpr/gqs,gqd->sgd/dot_general | solution.py:158
  97.7 0.8 fusion.87
  98.5 1.9 convolution_add_fusion.2
  102.3 1.1 copy.122
  103.4 1.0 constant_dynamic-slice_fusion.10
  104.5 2.6 %fusion.83 = f32[2,512,1024]{2,1,0:T(8,128)} fusion(bf16[2,1024,128]{1,2,0:T(8,128)(2,1)S(1)} %get-tuple-element.1009, bf16[512,2,128]{2,0,1:T(8,128)(2,1)S(1)} %copy.121), kind=kOutput, calls=%fused_computation.41.clone.1 | convolution fusion | flops 268435456 | bytes 4980736 | tf_op jit(solution)/shard_map/while/body/eval_jaxpr/gqd,gsd->gqs/dot_general | solution.py:112
  108.0 4.3 %fusion.84 = bf16[2,1024,512]{1,2,0:T(8,128)(2,1)S(1)} fusion(f32[2,512,1024]{2,1,0:T(8,128)} %fusion.83, bf16[2,1024,128]{1,2,0:T(8,128)(2,1)} %get-tuple-element.1012, f32[2,1024]{1,0:T(2,128)S(1)} %get-tuple-element.1013, f32[2,1024]{1,0:T(2,128)S(1)} %get-tuple-element.1010, pred[1024,512]{0,1:T(8,128)(4,1)} %bitcast.234, ...), kind=kOutput, calls=%fused_computation.28.clone.1 | convolution fusion | flops 275775488 | bytes 7618560 | tf_op jit(solution)/shard_map/while/body/eval_jaxpr/gqd,gsd->gqs/dot_general | solution.py:146
  112.3 0.8 fusion.86
  113.2 2.3 %fusion.85 = bf16[2,512,128]{1,2,0:T(8,128)(2,1)S(1)} fusion(bf16[2,1024,128]{1,2,0:T(8,128)(2,1)} %get-tuple-element.1012, f32[2,512,1024]{2,1,0:T(8,128)S(1)} %copy-done, f32[2,1024]{1,0:T(2,128)S(1)} %get-tuple-element.1010, pred[1024,512]{0,1:T(8,128)(4,1)S(1)} %bitcast.235), kind=kOutput, calls=%fused_computation.33.clone.1 | convolution fusion | flops 272629760 | bytes 5513216 | tf_op jit(solution)/shard_map/while/body/eval_jaxpr/gqs,gqd->sgd/dot_general | solution.py:158
  115.5 0.8 fusion.87
  116.4 3.1 %convolution_add_fusion.2 = f32[2,1024,128]{2,1,0:T(8,128)} fusion(bf16[2,1024,512]{1,2,0:T(8,128)(2,1)S(1)} %fusion.84, f32[2,1024,128]{2,1,0:T(8,128)} %get-tuple-element.983, pred[]{:T(512)S(6)} %compare.11, bf16[512,2,128]{2,0,1:T(8,128)(2,1)S(1)} %copy.121), kind=kOutput, calls=%fused_computation.36.clone.1 | convolution fusion | flops 268959744 | bytes 4456449 | tf_op jit(solution)/shard_map/while/body/eval_jaxpr/gqs,gsd->gqd/dot_general | solution.py:166
  119.5 2.3 %copy.86 = bf16[2,512,512]{2,1,0:T(8,128)(2,1)} copy(bf16[2,512,512]{1,2,0:T(8,128)(2,1)} %get-tuple-element.405) | data formatting | bytes 2097152 | tf_op jit(solution)/shard_map/convert_element_type | solution.py:177
  121.9 1.3 convert_element_type.42
  123.7 60.9 %reduce-scatter.2.cloned.1.call-done = bf16[128,512]{1,0:T(8,128)(2,1)} async-done(((bf16[1024,512]{1,0:T(8,128)(2,1)}), bf16[128,512]{1,0:T(8,128)(2,1)}) %reduce-scatter.2.cloned.1.call-update) | async-done | bytes 131088 | tf_op jit(solution)/shard_map/reduce_scatter | solution.py:176
  184.5 0.9 maximum_bitcast_fusion.1
  185.5 1.3 collective-permute-start.3
  187.5 1.0 broadcast_in_dim_reshape.4
  188.5 13.8 %collective-permute-done.3 = bf16[1,128,2560]{2,1,0:T(8,128)(2,1)S(1)} collective-permute-done((bf16[1,128,2560]{2,1,0:T(8,128)(2,1)S(1)}, bf16[1,128,2560]{2,1,0:T(8,128)(2,1)S(1)}, u32[]{:S(2)}, u32[]{:S(2)}) %collective-permute-start.3) | collective-permute-done | bytes 655392 | tf_op jit(solution)/shard_map/ppermute | solution.py:34
  202.3 0.8 slice.24
  (100 shorter events, 15.2 us)
Async XLA Ops:
  7.2 177.4 %reduce-scatter.2.cloned.1.call-start = ((), (), s32[]{:S(2)}) async-start(), calls=%async_computation.1 | async-start | bytes 1179648 | tf_op jit(solution)/shard_map/reduce_scatter | solution.py:176
  7.2 33.0 %collective-permute-start = (bf16[1,128,256]{2,1,0:T(8,128)(2,1)}, bf16[1,128,256]{2,1,0:T(8,128)(2,1)S(1)}, u32[]{:S(2)}, u32[]{:S(2)}) collective-permute-start(bf16[1,128,256]{2,1,0:T(8,128)(2,1)} %param.13), channel_id=1, source_target_pairs={{0,1},{1,0},{2,3},{3,2},{4,5},{5,4},{6,7},{7,6},{8,9},{9,8},{10,11... | collective-permute-start | bytes 196616 | tf_op jit(solution)/shard_map/ppermute | solution.py:24
  41.1 6.1 %collective-permute-start.1 = (bf16[2,128,256]{2,1,0:T(8,128)(2,1)S(1)}, bf16[2,128,256]{2,1,0:T(8,128)(2,1)S(1)}, u32[]{:S(2)}, u32[]{:S(2)}) collective-permute-start(bf16[2,128,256]{2,1,0:T(8,128)(2,1)S(1)} %get-tuple-element.665), channel_id=1, source_target_pairs={{0,2},{1,3},{2,0},{3,1},{4,6},{5,7},{6,4},{7,5},{8,10},{9,11},{10,... | collective-permute-start | bytes 393224 | tf_op jit(solution)/shard_map/ppermute | solution.py:24
  48.2 17.2 %collective-permute-start.2 = (bf16[4,128,256]{1,0,2:T(4,128)(2,1)}, bf16[4,128,256]{1,0,2:T(4,128)(2,1)}, u32[]{:S(2)}, u32[]{:S(2)}) collective-permute-start(bf16[4,128,256]{1,0,2:T(4,128)(2,1)} %copy.79), channel_id=1, source_target_pairs={{0,4},{1,5},{2,6},{3,7},{4,0},{5,1},{6,2},{7,3},{8,12},{9,13},{10,... | collective-permute-start | bytes 786440 | tf_op jit(solution)/shard_map/ppermute | solution.py:24
  49.0 14.4 %copy-start.4 = (bf16[1,128,2048]{2,1,0:T(8,128)(2,1)S(1)}, bf16[1,128,2048]{2,1,0:T(8,128)(2,1)}, u32[]{:S(2)}) copy-start(bf16[1,128,2048]{2,1,0:T(8,128)(2,1)} %param.14) | copy-start | bytes 1572868
  80.9 1.4 copy-start.2
  90.1 5.2 %copy-start = (f32[2,512,1024]{2,1,0:T(8,128)S(1)}, f32[2,512,1024]{2,1,0:T(8,128)}, u32[]{:S(2)}) copy-start(f32[2,512,1024]{2,1,0:T(8,128)} %fusion.83) | copy-start | bytes 12582916 | tf_op jit(solution)/shard_map/while
  90.2 5.2 %copy-start.1 = (pred[64,8,8,128]{3,1,2,0:T(8,128)(4,1)S(1)}, pred[64,8,8,128]{3,1,2,0:T(8,128)(4,1)}, u32[]{:S(2)}) copy-start(pred[64,8,8,128]{3,1,2,0:T(8,128)(4,1)} %copy.122) | copy-start | bytes 1572868 | tf_op jit(solution)/shard_map/while
  108.0 5.2 %copy-start = (f32[2,512,1024]{2,1,0:T(8,128)S(1)}, f32[2,512,1024]{2,1,0:T(8,128)}, u32[]{:S(2)}) copy-start(f32[2,512,1024]{2,1,0:T(8,128)} %fusion.83) | copy-start | bytes 12582916 | tf_op jit(solution)/shard_map/while
  108.0 5.2 %copy-start.1 = (pred[64,8,8,128]{3,1,2,0:T(8,128)(4,1)S(1)}, pred[64,8,8,128]{3,1,2,0:T(8,128)(4,1)}, u32[]{:S(2)}) copy-start(pred[64,8,8,128]{3,1,2,0:T(8,128)(4,1)} %copy.122) | copy-start | bytes 1572868 | tf_op jit(solution)/shard_map/while
  119.5 67.3 %copy-start.3 = (bf16[2,1024,128]{1,2,0:T(8,128)(2,1)S(1)}, bf16[2,1024,128]{1,2,0:T(8,128)(2,1)}, u32[]{:S(2)}) copy-start(bf16[2,1024,128]{1,2,0:T(8,128)(2,1)} %copy-done.2) | copy-start | bytes 1572868
  185.5 16.8 %collective-permute-start.3 = (bf16[1,128,2560]{2,1,0:T(8,128)(2,1)S(1)}, bf16[1,128,2560]{2,1,0:T(8,128)(2,1)S(1)}, u32[]{:S(2)}, u32[]{:S(2)}) collective-permute-start(bf16[1,128,2560]{2,1,0:T(8,128)(2,1)S(1)} %maximum_bitcast_fusion.1), channel_id=1, source_target_pairs={{8,0},{9,1},{10,2},{11,3},{12,4},{13,5},{14,6},{15,7},{24,16},{25,... | collective-permute-start | bytes 1966088 | tf_op jit(solution)/shard_map/ppermute | solution.py:34
Sparse Core Ops, SparseCore 0:
  122.0 62.5 reduce-scatter.1
